TPU v7x, 32 devices: a whole 2x2x4 slice. The times are simulated.
32 devices in a mesh: sec: 4 (over y, core), blk: 2 (over x), gy: 4 (over z).
Axes of the slice: x: 2, y: 2, z: 4, core: 2. Of those that a mesh axis runs over, the one named last changes fastest.
Arguments:
- normalized_kelvin: float32 [32, 64, 512], P('blk', 'gy', 'sec'), may hold values from 0.6 to 2
- co2_molar_part: float32 [32, 64, 512], P('blk', 'gy', 'sec'), may hold values from 0.02 to 0.2
- h2o_molar_part: float32 [32, 64, 512], P('blk', 'gy', 'sec'), may hold values from 0.02 to 0.25
- particulate_scaled: float32 [32, 64, 512], P('blk', 'gy', 'sec'), may hold values from 0.01 to 1
- region_local_subgrids: int32 [4, 2, 4, 512], P('sec', 'blk', 'gy'), may hold values from 0 to 511, each once within a row
- entry_target_tile: int32 [64, 5], P(('sec', 'blk', 'gy')), may hold values from 0 to 63, as said below
- nonempty_entries_per_strip: int32 [64], P(('sec', 'blk', 'gy')), may hold values from 1 to 5, as said below
- transfer_matrix_tiles: bfloat16 [64, 5, 256, 256], P(('sec', 'blk', 'gy')), may hold values from -0.15625 to 0.15625
Outputs:
- temperature_new: float32 [32, 64, 512], P('blk', 'gy', 'sec')
- carbon_dioxide_new: float32 [32, 64, 512], P('blk', 'gy', 'sec')
- water_new: float32 [32, 64, 512], P('blk', 'gy', 'sec')
- soot_new: float32 [32, 64, 512], P('blk', 'gy', 'sec')
- source: float32 [32, 64, 512], P('blk', 'gy', 'sec')
Inputs may be any that keep to these rules, and one draw needn't show every extreme that they name: `region_local_subgrids`: each device's row is a permutation of its 512 boxes. `entry_target_tile`: slot 0 of block row r names r itself; slots at or beyond the row's count are not read. `nonempty_entries_per_strip`: some block row has 5 live slots and some has 1.
All inputs are finite; a program needn't handle non-finite values.
Results may differ from a plain program's by a relative error of at most 0.0018.
Values may be sent and summed in bfloat16 or wider, within the bound.
A program may use at most 64 MiB of HBM per device.

v0:
```python
import jax
import jax.numpy as jnp
from jax import lax
from jax.sharding import PartitionSpec as P

BOX = 4


diffusion_rates = (0.12, 0.1, 0.1, 0.02)
vapour_attenuation_rate = (0.4, 1.6, 6.4, 25.6)
mixture_share_offset = (0.3, 0.25, 0.2, 0.15)
mixture_share_slope = (-0.05, 0.02, 0.03, 0.01)
particulate_attenuation_rate = 1.5
radiance_multiplier = 0.05
heating_rate = 0.1


def extended(block, sides, width):
    for axis, dim in sides:
        count = lax.axis_size(axis)
        forward = [(i, i + 1) for i in range(count - 1)]
        backward = [(target, source) for source, target in forward]
        low = lax.ppermute(
            lax.slice_in_dim(block, block.shape[dim] - width, None, axis=dim), axis, forward
        )
        high = lax.ppermute(lax.slice_in_dim(block, 0, width, axis=dim), axis, backward)
        block = jnp.concatenate([low, block, high], axis=dim)
    return block


def radiant_output_of_region(normalized_kelvin, co2_molar_part, h2o_molar_part, particulate_scaled):
    molecular_constituents = co2_molar_part + h2o_molar_part
    overall_summation = jnp.zeros_like(normalized_kelvin)
    for region_position in range(4):
        greybody_share = (
            mixture_share_offset[region_position]
            + mixture_share_slope[region_position] * normalized_kelvin
        )
        overall_summation = overall_summation + greybody_share * (
            vapour_attenuation_rate[region_position] * molecular_constituents
            + particulate_attenuation_rate * particulate_scaled * normalized_kelvin
        )
    kelvin_tesseract = normalized_kelvin * normalized_kelvin * normalized_kelvin * normalized_kelvin
    return radiance_multiplier * kelvin_tesseract * overall_summation


def diffuse(constituent_arrays, padded):
    beside = padded[:, 2:, 1:-1, 1:-1] + padded[:, :-2, 1:-1, 1:-1]
    beside = beside + padded[:, 1:-1, 2:, 1:-1] + padded[:, 1:-1, :-2, 1:-1]
    beside = beside + padded[:, 1:-1, 1:-1, 2:] + padded[:, 1:-1, 1:-1, :-2]
    rates = jnp.array(diffusion_rates, jnp.float32)[:, None, None, None]
    return constituent_arrays + rates * (beside - 6.0 * constituent_arrays)


def local(
    normalized_kelvin,
    co2_molar_part,
    h2o_molar_part,
    particulate_scaled,
    region_local_subgrids,
    entry_target_tile,
    nonempty_entries_per_strip,
    transfer_matrix_tiles,
):
    constituent_arrays = jnp.stack(
        [normalized_kelvin, co2_molar_part, h2o_molar_part, particulate_scaled]
    )
    padded = extended(constituent_arrays, (("sec", 3), ("blk", 1), ("gy", 2)), 1)
    swept = diffuse(constituent_arrays, padded)
    region_extent_third, region_extent_second, domain_span_leading = normalized_kelvin.shape
    radiated_energy_rate = radiant_output_of_region(
        normalized_kelvin, co2_molar_part, h2o_molar_part, particulate_scaled
    )
    shaped = radiated_energy_rate.reshape(
        region_extent_third // BOX,
        BOX,
        region_extent_second // BOX,
        BOX,
        domain_span_leading // BOX,
        BOX,
    )
    box_emission = (jnp.sum(shaped, axis=(1, 3, 5)) * (1.0 / (BOX * BOX * BOX))).reshape(-1)
    box_order = region_local_subgrids.reshape(-1)
    zone_emission = box_emission[box_order]
    block_count = transfer_matrix_tiles.shape[0]
    slot_count = transfer_matrix_tiles.shape[1]
    zone_size = transfer_matrix_tiles.shape[2]
    emitted = zone_emission.astype(jnp.bfloat16).reshape(block_count, zone_size)
    shard_rows = lax.all_gather(emitted, ("sec", "blk", "gy"), axis=0, tiled=True)
    shard_len = shard_rows.shape[0]
    offsets = jnp.arange(shard_len, dtype=jnp.int32)[None, None, :]
    wanted = (entry_target_tile[:, :, None] == offsets).astype(jnp.bfloat16)
    collected = jnp.einsum("rkn,nj->rkj", wanted, shard_rows, preferred_element_type=jnp.float32)
    live_slots = (
        jnp.arange(slot_count, dtype=jnp.int32)[None, :] < nonempty_entries_per_strip[:, None]
    )
    picked = jnp.where(live_slots[:, :, None], collected, 0.0).astype(jnp.bfloat16)
    taken_in_light = jnp.einsum(
        "rkij,rkj->ri", transfer_matrix_tiles, picked, preferred_element_type=jnp.float32
    )
    net_zone = taken_in_light.reshape(-1) - zone_emission
    box_net = jnp.zeros_like(net_zone).at[box_order].set(net_zone)
    box_grid = box_net.reshape(
        region_extent_third // BOX, 1, region_extent_second // BOX, 1, domain_span_leading // BOX, 1
    )
    source = jnp.broadcast_to(
        box_grid,
        (
            region_extent_third // BOX,
            BOX,
            region_extent_second // BOX,
            BOX,
            domain_span_leading // BOX,
            BOX,
        ),
    ).reshape(region_extent_third, region_extent_second, domain_span_leading)
    return (swept[0] + heating_rate * source, swept[1], swept[2], swept[3], source)


def solution(mesh):
    placed = (
        P("blk", "gy", "sec"),
        P("blk", "gy", "sec"),
        P("blk", "gy", "sec"),
        P("blk", "gy", "sec"),
        P("sec", "blk", "gy", None),
        P(("sec", "blk", "gy"), None),
        P(("sec", "blk", "gy")),
        P(("sec", "blk", "gy"), None, None, None),
    )
    return jax.shard_map(
        local,
        mesh=mesh,
        in_specs=placed,
        out_specs=(
            P("blk", "gy", "sec"),
            P("blk", "gy", "sec"),
            P("blk", "gy", "sec"),
            P("blk", "gy", "sec"),
            P("blk", "gy", "sec"),
        ),
        check_vma=False,
    )
```

profile of v0, /device:TPU:0, one launch (start us, length us, event | category | flops | bytes accessed | tf_op | source)
XLA Modules:
  0.0 121.7 jit_solution(14417583017567707316)
XLA Ops:
  0.6 0.0 copy-start
  0.6 1.2 %pad_maximum_fusion.35 = f32[4,16,16,128]{3,2,1,0:T(8,128)S(1)} fusion(f32[1,16,16,128]{3,2,1,0:T(8,128)} %bitcast.43, f32[1,16,16,128]{3,2,1,0:T(8,128)} %bitcast.28, f32[1,16,16,128]{3,2,1,0:T(8,128)} %bitcast.33, f32[1,16,16,128]{3,2,1,0:T(8,128)} %bitcast.38), kind=kLoop, calls=%fused_computation.48 | loop fusion | flops 393216 | bytes 1048576 | tf_op jit(solution)/shard_map/stack | solution.py:65
  1.9 0.0 copy-start.1
  1.9 0.0 copy-start.2
  1.9 0.0 copy-start.3
  1.9 0.0 copy-start.4
  1.9 0.0 copy-start.6
  1.9 1.0 fusion.19
  3.0 2.4 %collective-permute-start = (f32[4,16,16,1]{3,2,1,0:T(8,128)}, f32[4,16,16,1]{3,2,1,0:T(8,128)S(1)}, u32[]{:S(2)}, u32[]{:S(2)}) collective-permute-start(f32[4,16,16,1]{3,2,1,0:T(8,128)} %get-tuple-element.13), channel_id=1, source_target_pairs={{0,8},{8,16},{16,24},{1,9},{9,17},{17,25},{2,10},{10,18},{18,26},{... | collective-permute-start | bytes 12296 | tf_op jit(solution)/shard_map/ppermute | solution.py:23
  5.3 1.3 %collective-permute-start.1 = (f32[4,16,16,1]{3,2,1,0:T(8,128)S(1)}, f32[4,16,16,1]{3,2,1,0:T(8,128)S(1)}, u32[]{:S(2)}, u32[]{:S(2)}) collective-permute-start(f32[4,16,16,1]{3,2,1,0:T(8,128)S(1)} %get-tuple-element.12), channel_id=1, source_target_pairs={{8,0},{16,8},{24,16},{9,1},{17,9},{25,17},{10,2},{18,10},{26,18},{... | collective-permute-start | bytes 12296 | tf_op jit(solution)/shard_map/ppermute | solution.py:26
  6.6 0.0 copy-done.1
  6.7 0.0 copy-done.2
  6.7 0.0 copy-done.3
  6.7 0.0 copy-done.4
  6.7 0.1 fusion.11
  6.8 0.0 copy-done.6
  6.9 5.7 %reshape.83 = f32[4,4,4,4,32,4]{5,4,3,2,1,0:T(8,128)} reshape(f32[16,16,128]{2,1,0:T(8,128)S(1)} %fusion.11) | data formatting | bytes 262144 | tf_op jit(solution)/shard_map/reshape | solution.py:74
  12.5 2.6 %reduce_sum.9 = f32[4,4,32]{2,1,0:T(4,128)S(1)} reduce(f32[4,4,4,4,32,4]{5,4,3,2,1,0:T(8,128)} %reshape.83, f32[]{:T(128)} %constant.1.clone.1), dimensions={1,3,5}, to_apply=%region_0.0 | reduce | flops 32256 | bytes 133124 | tf_op jit(solution)/shard_map/reduce_sum | solution.py:82
  15.2 0.0 copy-start.9
  15.2 0.0 copy-start.8
  15.2 0.1 mul.154
  15.3 3.5 %gather_fusion = f32[512]{0:T(512)S(1)} fusion(f32[512]{0:T(512)S(1)} %mul.154, s32[1024]{0:T(1024)S(1)} %pad_clamp_fusion), kind=kCustom, calls=%fused_computation | custom fusion | bytes 6144 | tf_op jit(solution)/shard_map/gather | solution.py:84
  18.8 70.7 %all-gather = bf16[32,2,256]{2,1,0:T(2,128)(2,1)S(1)} all-gather(bf16[1,2,256]{2,1,0:T(2,128)(2,1)S(1)} %reshape.102), channel_id=1, replica_groups=mesh['sec'=4,'blk'=2,'gy'=4] {'sec','blk','gy'}, dimensions={0}, use_global_device_ids=true | all-gather | bytes 33792 | tf_op jit(solution)/shard_map/all_gather | solution.py:89
  89.5 0.0 copy-done.9
  89.5 0.1 iota_compare_fusion.2
  89.5 0.0 copy-done.8
  89.5 0.2 fusion.1
  89.7 0.0 collective-permute-done
  89.7 0.0 collective-permute-done.1
  89.8 0.1 pad_maximum_fusion.36
  89.9 1.3 %collective-permute-start.2 = (f32[4,1,16,130]{3,2,1,0:T(8,128)S(1)}, f32[4,1,16,130]{3,2,1,0:T(8,128)S(1)}, u32[]{:S(2)}, u32[]{:S(2)}) collective-permute-start(f32[4,1,16,130]{3,2,1,0:T(8,128)S(1)} %get-tuple-element.6), channel_id=1, source_target_pairs={{4,0},{5,1},{6,2},{7,3},{12,8},{13,9},{14,10},{15,11},{20,16},{21,... | collective-permute-start | bytes 99848 | tf_op jit(solution)/shard_map/ppermute | solution.py:26
  91.2 4.5 %collective-permute-start.3 = (f32[4,1,16,130]{3,2,1,0:T(8,128)S(1)}, f32[4,1,16,130]{3,2,1,0:T(8,128)S(1)}, u32[]{:S(2)}, u32[]{:S(2)}) collective-permute-start(f32[4,1,16,130]{3,2,1,0:T(8,128)S(1)} %get-tuple-element.5), channel_id=1, source_target_pairs={{0,4},{1,5},{2,6},{3,7},{8,12},{9,13},{10,14},{11,15},{16,20},{17,... | collective-permute-start | bytes 99848 | tf_op jit(solution)/shard_map/ppermute | solution.py:23
  95.7 0.0 copy-done
  95.7 0.4 fusion.13
  96.2 0.0 collective-permute-done.2
  96.2 1.4 %collective-permute-done.3 = f32[4,1,16,130]{3,2,1,0:T(8,128)S(1)} collective-permute-done((f32[4,1,16,130]{3,2,1,0:T(8,128)S(1)}, f32[4,1,16,130]{3,2,1,0:T(8,128)S(1)}, u32[]{:S(2)}, u32[]{:S(2)}) %collective-permute-start.3) | collective-permute-done | bytes 33312 | tf_op jit(solution)/shard_map/ppermute | solution.py:23
  97.6 0.5 pad_maximum_fusion.2
  98.1 0.1 fusion.18
  98.2 1.3 %collective-permute-start.4 = (f32[4,18,1,130]{3,2,1,0:T(1,128)S(1)}, f32[4,18,1,130]{3,2,1,0:T(1,128)S(1)}, u32[]{:S(2)}, u32[]{:S(2)}) collective-permute-start(f32[4,18,1,130]{3,2,1,0:T(1,128)S(1)} %get-tuple-element.7), channel_id=1, source_target_pairs={{1,0},{2,1},{3,2},{5,4},{6,5},{7,6},{9,8},{10,9},{11,10},{13,12},{... | collective-permute-start | bytes 112328 | tf_op jit(solution)/shard_map/ppermute | solution.py:26
  99.5 4.5 %collective-permute-start.5 = (f32[4,18,1,130]{3,2,1,0:T(1,128)S(1)}, f32[4,18,1,130]{3,2,1,0:T(1,128)S(1)}, u32[]{:S(2)}, u32[]{:S(2)}) collective-permute-start(f32[4,18,1,130]{3,2,1,0:T(1,128)S(1)} %get-tuple-element.8), channel_id=1, source_target_pairs={{0,1},{1,2},{2,3},{4,5},{5,6},{6,7},{8,9},{9,10},{10,11},{12,13},{... | collective-permute-start | bytes 112328 | tf_op jit(solution)/shard_map/ppermute | solution.py:23
  104.1 2.4 %pad_maximum_fusion = (f32[4,18,17,130]{3,2,1,0:T(8,128)}, f32[4,18,17,130]{3,2,1,0:T(8,128)}) fusion(f32[1,16,16,128]{3,2,1,0:T(8,128)S(1)} %bitcast.31, f32[1,16,16,128]{3,2,1,0:T(8,128)S(1)} %bitcast.36, f32[1,16,16,128]{3,2,1,0:T(8,128)S(1)} %bitcast.41), kind=kLoop, calls=%fused_computation.2 | loop fusion | flops 636480 | bytes 1666176 | tf_op jit(solution)/shard_map/stack | solution.py:65
  106.4 2.4 %scatter_custom_fusion = f32[512]{0:T(512)S(1)} fusion(s32[512]{0:T(512)S(1)} %bitcast.48, f32[512]{0:T(512)S(1)} %sub.7, f32[]{:T(128)} %constant.1.clone.1), kind=kCustom, calls=%fused_computation.72 | custom fusion | bytes 2052 | tf_op jit(solution)/shard_map/scatter | solution.py:102
  108.9 0.1 broadcast_in_dim.33
  109.0 2.6 %broadcast_in_dim.34 = f32[4,4,4,4,32,4]{5,4,3,2,1,0:T(8,128)} broadcast(f32[4,4,32]{2,1,0:T(4,128)S(1)} %broadcast_in_dim.33), dimensions={0,2,4} | broadcast | bytes 133120 | tf_op jit(solution)/shard_map/broadcast_in_dim | solution.py:106
  111.5 0.0 copy-start.7
  111.5 4.9 %reshape.85 = f32[16,16,128]{2,1,0:T(8,128)S(1)} reshape(f32[4,4,4,4,32,4]{5,4,3,2,1,0:T(8,128)} %broadcast_in_dim.34) | data formatting | bytes 262144 | tf_op jit(solution)/shard_map/reshape | solution.py:116
  116.4 0.0 copy-start.5
  116.4 0.0 collective-permute-done.4
  116.4 0.0 collective-permute-done.5
  116.4 0.0 copy-done.7
  116.4 3.8 %fusion.5 = f32[4,16,16,128]{3,2,1,0:T(8,128)S(1)} fusion(f32[4,16,16,1]{3,2,1,0:T(8,128)S(1)} %collective-permute-done, f32[1,16,16,128]{3,2,1,0:T(8,128)S(1)} %bitcast.46, f32[1,16,16,128]{3,2,1,0:T(8,128)S(1)} %bitcast.32, f32[1,16,16,128]{3,2,1,0:T(8,128)S(1)} %bitcast.37, f32[1,16,16,128]{3,2,1,0:T(8,128)S(1)} %bitcast.42, ...), kind=kLoop, calls=%fused_computation.12 | loop fusion | flops 5767168 | bytes 2246800 | tf_op jit(solution)/shard_map/add | solution.py:52
  120.3 0.8 slice_bitcast_fusion
  121.0 0.0 copy-done.5
  121.0 0.7 fusion.12
  (9 shorter events, 0.1 us)
Async XLA Ops:
  0.6 95.1 %copy-start = (bf16[2,5,256,256]{3,2,1,0:T(8,128)(2,1)S(1)}, bf16[2,5,256,256]{3,2,1,0:T(8,128)(2,1)}, u32[]{:S(2)}) copy-start(bf16[2,5,256,256]{3,2,1,0:T(8,128)(2,1)} %param.16) | copy-start | bytes 3932164
  1.9 4.8 %copy-start.1 = (f32[16,16,128]{2,1,0:T(8,128)S(1)}, f32[16,16,128]{2,1,0:T(8,128)}, u32[]{:S(2)}) copy-start(f32[16,16,128]{2,1,0:T(8,128)} %param.11) | copy-start | bytes 393220
  1.9 4.8 %copy-start.2 = (f32[16,16,128]{2,1,0:T(8,128)S(1)}, f32[16,16,128]{2,1,0:T(8,128)}, u32[]{:S(2)}) copy-start(f32[16,16,128]{2,1,0:T(8,128)} %param.10) | copy-start | bytes 393220
  1.9 4.8 %copy-start.3 = (f32[16,16,128]{2,1,0:T(8,128)S(1)}, f32[16,16,128]{2,1,0:T(8,128)}, u32[]{:S(2)}) copy-start(f32[16,16,128]{2,1,0:T(8,128)} %param.9) | copy-start | bytes 393220
  1.9 4.8 %copy-start.4 = (f32[16,16,128]{2,1,0:T(8,128)S(1)}, f32[16,16,128]{2,1,0:T(8,128)}, u32[]{:S(2)}) copy-start(f32[16,16,128]{2,1,0:T(8,128)} %param.12) | copy-start | bytes 393220
  1.9 4.9 %copy-start.6 = (s32[1,1,1,512]{3,2,1,0:T(1,128)S(1)}, s32[1,1,1,512]{3,2,1,0:T(1,128)}, u32[]{:S(2)}) copy-start(s32[1,1,1,512]{3,2,1,0:T(1,128)} %param.13) | copy-start | bytes 6148
  3.0 86.8 %collective-permute-start = (f32[4,16,16,1]{3,2,1,0:T(8,128)}, f32[4,16,16,1]{3,2,1,0:T(8,128)S(1)}, u32[]{:S(2)}, u32[]{:S(2)}) collective-permute-start(f32[4,16,16,1]{3,2,1,0:T(8,128)} %get-tuple-element.13), channel_id=1, source_target_pairs={{0,8},{8,16},{16,24},{1,9},{9,17},{17,25},{2,10},{10,18},{18,26},{... | collective-permute-start | bytes 12296 | tf_op jit(solution)/shard_map/ppermute | solution.py:23
  5.3 84.4 %collective-permute-start.1 = (f32[4,16,16,1]{3,2,1,0:T(8,128)S(1)}, f32[4,16,16,1]{3,2,1,0:T(8,128)S(1)}, u32[]{:S(2)}, u32[]{:S(2)}) collective-permute-start(f32[4,16,16,1]{3,2,1,0:T(8,128)S(1)} %get-tuple-element.12), channel_id=1, source_target_pairs={{8,0},{16,8},{24,16},{9,1},{17,9},{25,17},{10,2},{18,10},{26,18},{... | collective-permute-start | bytes 12296 | tf_op jit(solution)/shard_map/ppermute | solution.py:26
  15.2 74.3 %copy-start.9 = (s32[2]{0:T(128)S(1)}, s32[2]{0:T(128)}, u32[]{:S(2)}) copy-start(s32[2]{0:T(128)} %param.15) | copy-start | bytes 28
  15.2 74.4 %copy-start.8 = (s32[2,5]{1,0:T(2,128)S(1)}, s32[2,5]{1,0:T(2,128)}, u32[]{:S(2)}) copy-start(s32[2,5]{1,0:T(2,128)} %param.14) | copy-start | bytes 124
  89.9 6.3 %collective-permute-start.2 = (f32[4,1,16,130]{3,2,1,0:T(8,128)S(1)}, f32[4,1,16,130]{3,2,1,0:T(8,128)S(1)}, u32[]{:S(2)}, u32[]{:S(2)}) collective-permute-start(f32[4,1,16,130]{3,2,1,0:T(8,128)S(1)} %get-tuple-element.6), channel_id=1, source_target_pairs={{4,0},{5,1},{6,2},{7,3},{12,8},{13,9},{14,10},{15,11},{20,16},{21,... | collective-permute-start | bytes 99848 | tf_op jit(solution)/shard_map/ppermute | solution.py:26
  91.2 6.4 %collective-permute-start.3 = (f32[4,1,16,130]{3,2,1,0:T(8,128)S(1)}, f32[4,1,16,130]{3,2,1,0:T(8,128)S(1)}, u32[]{:S(2)}, u32[]{:S(2)}) collective-permute-start(f32[4,1,16,130]{3,2,1,0:T(8,128)S(1)} %get-tuple-element.5), channel_id=1, source_target_pairs={{0,4},{1,5},{2,6},{3,7},{8,12},{9,13},{10,14},{11,15},{16,20},{17,... | collective-permute-start | bytes 99848 | tf_op jit(solution)/shard_map/ppermute | solution.py:23
  98.2 18.2 %collective-permute-start.4 = (f32[4,18,1,130]{3,2,1,0:T(1,128)S(1)}, f32[4,18,1,130]{3,2,1,0:T(1,128)S(1)}, u32[]{:S(2)}, u32[]{:S(2)}) collective-permute-start(f32[4,18,1,130]{3,2,1,0:T(1,128)S(1)} %get-tuple-element.7), channel_id=1, source_target_pairs={{1,0},{2,1},{3,2},{5,4},{6,5},{7,6},{9,8},{10,9},{11,10},{13,12},{... | collective-permute-start | bytes 112328 | tf_op jit(solution)/shard_map/ppermute | solution.py:26
  99.5 16.9 %collective-permute-start.5 = (f32[4,18,1,130]{3,2,1,0:T(1,128)S(1)}, f32[4,18,1,130]{3,2,1,0:T(1,128)S(1)}, u32[]{:S(2)}, u32[]{:S(2)}) collective-permute-start(f32[4,18,1,130]{3,2,1,0:T(1,128)S(1)} %get-tuple-element.8), channel_id=1, source_target_pairs={{0,1},{1,2},{2,3},{4,5},{5,6},{6,7},{8,9},{9,10},{10,11},{12,13},{... | collective-permute-start | bytes 112328 | tf_op jit(solution)/shard_map/ppermute | solution.py:23
  111.5 4.9 %copy-start.7 = (f32[4]{0:T(128)S(1)}, f32[4]{0:T(128)}, u32[]{:S(2)}) copy-start(f32[4]{0:T(128)} %constant.20.clone) | copy-start | bytes 52
  116.4 4.6 %copy-start.5 = (f32[16,16,128]{2,1,0:T(8,128)}, f32[16,16,128]{2,1,0:T(8,128)S(1)}, u32[]{:S(2)}) copy-start(f32[16,16,128]{2,1,0:T(8,128)S(1)} %reshape.85) | copy-start | bytes 393220
where the time goes:
time: 122 us
  blocking collectives  70.7 us (58%)
  local copies, waits for them, and re-layouts  21.2 us (17%)
  starting transfers between devices  15.4 us (13%)
  other arithmetic  11.6 us (10%)
  waiting for transfers between devices  1.45 us (1%)
    all_gather x1, blocking collectives, local(): lax.all_gather(emitted, ('sec', 'blk', 'gy'), axis=0, tiled=True)  70.7 us
    ppermute x3, starting transfers between devices, extended(): lax.ppermute(lax.slice_in_dim(block, block.shape[dim] - width, None, axis...  11.5 us
    reshape x1, local copies, waits for them, and re-layouts, local(): radiated_energy_rate.reshape(region_extent_third // BOX, BOX, region_exte...  5.68 us
    reshape x1, local copies, waits for them, and re-layouts, local(): source = jnp.broadcast_to(box_grid, (region_extent_third // BOX, BOX, reg...  4.87 us
    ppermute x3, starting transfers between devices, extended(): lax.ppermute(lax.slice_in_dim(block, 0, width, axis=dim), axis, backward)  3.88 us
    add x1, other arithmetic, diffuse(): return constituent_arrays + rates * (beside - 6.0 * constituent_arrays)  3.84 us
    another operation x2, other arithmetic, local(): jnp.stack([normalized_kelvin, co2_molar_part, h2o_molar_part, particulate...  3.6 us
    gather x1, local copies, waits for them, and re-layouts, local(): zone_emission = box_emission[box_order]  3.48 us
  transfers between devices with their start and end apart: 6, of which 1 were waited for; matrix products, arithmetic and copies ran while one was open for 21% of the time, Pallas kernels for 0%

commit v1 on v0

v1 whole, which is shorter than its diff:
```python
import functools

import jax
import jax.numpy as jnp
from jax import lax
from jax.experimental import pallas as pl
from jax.experimental.pallas import tpu as pltpu
from jax.sharding import PartitionSpec as P

BOX = 4
AXES = ("sec", "blk", "gy")

diffusion_rates = (0.12, 0.1, 0.1, 0.02)
vapour_attenuation_rate = (0.4, 1.6, 6.4, 25.6)
mixture_share_offset = (0.3, 0.25, 0.2, 0.15)
mixture_share_slope = (-0.05, 0.02, 0.03, 0.01)
particulate_attenuation_rate = 1.5
radiance_multiplier = 0.05
heating_rate = 0.1

SHARE_OFFSET = sum(mixture_share_offset)
SHARE_SLOPE = sum(mixture_share_slope)
VAPOUR_OFFSET = sum(b * k for b, k in zip(mixture_share_offset, vapour_attenuation_rate))
VAPOUR_SLOPE = sum(c * k for c, k in zip(mixture_share_slope, vapour_attenuation_rate))

MESH = pl.DeviceIdType.MESH
NT = (((1,), (1,)), ((), ()))
TN = (((0,), (0,)), ((), ()))


def iota(shape, dim):
    return lax.broadcasted_iota(jnp.int32, shape, dim)


def group_sum(value, axis):
    size = value.shape[axis]
    place = iota(value.shape, axis)
    for step in (1, 2):
        above = pltpu.roll(value, size - step, axis)
        below = pltpu.roll(value, step, axis)
        value = value + jnp.where((place & step) == 0, above, below)
    return value


def kernel(
    dims,
    counts,
    kelvin_hbm,
    co2_hbm,
    h2o_hbm,
    soot_hbm,
    order_hbm,
    tile_ref,
    live_ref,
    matrix_hbm,
    *rest,
):
    outs = rest[:5]
    (
        fields,
        order_ref,
        matrix,
        done,
        gathered,
        z_out,
        y_out,
        x_out,
        z_in,
        y_in,
        x_in,
        in_sem,
        out_sem,
        face_send,
        face_recv,
        send_sem,
        recv_sem,
    ) = rest[5:]
    cz, cy, cx = dims
    n_sec, n_blk, n_gy = counts
    cells = cz * cy
    rows = matrix.shape[0]
    slots = matrix.shape[1]
    zones = order_ref.shape[1]
    zone = zones // rows
    n_plane = n_blk * n_gy
    sec, blk, gy = (lax.axis_index(a) for a in AXES)
    plane = blk * n_gy + gy
    me = sec * n_plane + plane

    copies = [
        pltpu.make_async_copy(src, fields.at[i], in_sem.at[i])
        for i, src in enumerate((kelvin_hbm, co2_hbm, h2o_hbm, soot_hbm))
    ]
    copies.append(pltpu.make_async_copy(order_hbm, order_ref, in_sem.at[4]))
    copies.append(pltpu.make_async_copy(matrix_hbm, matrix, in_sem.at[5]))
    for copy in copies:
        copy.start()

    def plane_peer(i):
        flat = lax.rem(plane + i, n_plane)
        return {"blk": lax.div(flat, n_gy), "gy": lax.rem(flat, n_gy)}

    def sec_peer(i):
        return {"sec": lax.rem(sec + i, n_sec)}

    def each(count, body):
        if count <= 32:
            for i in range(1, count):
                body(i)
        else:
            lax.fori_loop(1, count, lambda i, c: (body(i), c)[1], 0)

    barrier = pltpu.get_barrier_semaphore()
    for count, peer in ((n_plane, plane_peer), (n_sec, sec_peer)):
        each(
            count,
            lambda i, peer=peer: pl.semaphore_signal(
                barrier, inc=1, device_id=peer(i), device_id_type=MESH
            ),
        )

    places = (("sec", sec, n_sec), ("blk", blk, n_blk), ("gy", gy, n_gy))
    landing = (x_in, z_in, y_in)
    leaving = (x_out, z_out, y_out)
    for (_, at, size), land in zip(places, landing):
        for side, edge in ((0, 0), (1, size - 1)):

            @pl.when(at == edge)
            def _(land=land, side=side):
                land[side] = jnp.zeros(land.shape[1:], land.dtype)

    for copy in copies[:5]:
        copy.wait()

    kelvin = fields[0]
    vapour = fields[1] + fields[2]
    soot_kelvin = fields[3] * kelvin
    share = vapour * (VAPOUR_OFFSET + VAPOUR_SLOPE * kelvin) + (
        particulate_attenuation_rate * soot_kelvin * (SHARE_OFFSET + SHARE_SLOPE * kelvin)
    )
    squared = kelvin * kelvin
    emission = radiance_multiplier * (squared * squared) * share
    slabs = emission.reshape(cz // BOX, BOX, cy, cx)
    slabs = (slabs[:, 0] + slabs[:, 1] + slabs[:, 2] + slabs[:, 3]).reshape(cells // BOX, cx)
    box_mean = group_sum(group_sum(slabs, 0), 1) * (1.0 / (BOX * BOX * BOX))

    order = order_ref[...]
    across = cx // BOX
    x_shape = (cx, zones)
    r_shape = (cells // BOX, zones)
    x_at = iota(x_shape, 0)
    r_at = iota(r_shape, 0)
    same_x = lax.rem(order, across) == lax.div(x_at, BOX)
    box_row = lax.div(r_at, cy) * (cy // BOX) + lax.div(lax.rem(r_at, cy), BOX)
    same_r = lax.div(order, across) == box_row
    pick_x = jnp.where(same_x & (lax.rem(x_at, BOX) == 0), 1.0, 0.0).astype(jnp.bfloat16)
    pick_r = same_r & (lax.rem(r_at, BOX) == 0)
    by_row = jnp.dot(box_mean.astype(jnp.bfloat16), pick_x, preferred_element_type=jnp.float32)
    emitted = jnp.sum(jnp.where(pick_r, by_row, 0.0), axis=0, keepdims=True)
    for r in range(rows):
        gathered[me * rows + r] = emitted[:, r * zone : (r + 1) * zone]

    lane = iota((cells, cx), 1)
    packed = jnp.zeros((cells, cx), jnp.float32)
    for f in range(4):
        field = fields.at[f]
        z_out[0, f] = field[pl.ds(0, cy), :]
        z_out[1, f] = field[pl.ds(cells - cy, cy), :]
        y_out[0, f] = field[pl.ds(0, cz, stride=cy), :]
        y_out[1, f] = field[pl.ds(cy - 1, cz, stride=cy), :]
        packed = jnp.where((lane >> 1) == f, pltpu.roll(field[...], 2 * f + 1, 1), packed)
    x_out[...] = jnp.transpose(packed)[:8]

    pl.semaphore_wait(barrier, n_plane - 1 + n_sec - 1)

    def push(start, length, peer, stage):
        block = gathered.at[pl.ds(start, length)]
        pltpu.make_async_remote_copy(
            src_ref=block,
            dst_ref=block,
            send_sem=send_sem.at[stage],
            recv_sem=recv_sem.at[stage],
            device_id=peer,
            device_id_type=MESH,
        ).start()

    def settle(length, sem):
        block = gathered.at[pl.ds(0, length)]
        pltpu.make_async_copy(block, block, sem).wait()

    each(n_plane, lambda i: push(me * rows, rows, plane_peer(i), 0))

    def face(which, side):
        axis, at, _ = places[which]
        source = x_out if which == 0 else leaving[which].at[side]
        return pltpu.make_async_remote_copy(
            src_ref=source,
            dst_ref=landing[which].at[1 - side],
            send_sem=face_send.at[which, side],
            recv_sem=face_recv.at[which, 1 - side],
            device_id={axis: at + (2 * side - 1)},
            device_id_type=MESH,
        )

    def has(which, side):
        _, at, size = places[which]
        return at > 0 if side == 0 else at < size - 1

    for which in (1, 2, 0):
        for side in (0, 1):

            @pl.when(has(which, side))
            def _(which=which, side=side):
                face(which, side).start()

    place = iota((cells, cx), 0)
    y_place = lax.rem(place, cy)
    for f in range(4):
        value = fields[f]
        total = jnp.where(place >= cy, pltpu.roll(value, cy, 0), 0.0)
        total += jnp.where(place < cells - cy, pltpu.roll(value, cells - cy, 0), 0.0)
        total += jnp.where(y_place > 0, pltpu.roll(value, 1, 0), 0.0)
        total += jnp.where(y_place < cy - 1, pltpu.roll(value, cells - 1, 0), 0.0)
        total += jnp.where(lane > 0, pltpu.roll(value, 1, 1), 0.0)
        total += jnp.where(lane < cx - 1, pltpu.roll(value, cx - 1, 1), 0.0)
        done[f] = value + diffusion_rates[f] * (total - 6.0 * value)

    settle((n_plane - 1) * rows, recv_sem.at[0])
    each(n_sec, lambda i: push(sec * n_plane * rows, n_plane * rows, sec_peer(i), 1))

    for which in (0, 1, 2):
        for side in (0, 1):

            @pl.when(has(which, side))
            def _(which=which, side=side):
                face(which, 1 - side).wait_recv()

    shape = (16, 4 * cx)
    row, column = iota(shape, 0), iota(shape, 1)
    chosen = ((row < 8) & (column == (row >> 1) * cx) & ((row & 1) == 0)) | (
        (row >= 8) & (column == ((row - 8) >> 1) * cx + cx - 1) & ((row & 1) == 1)
    )
    sides = jnp.concatenate([x_in[0], x_in[1]], axis=0)
    x_add = lax.dot_general(
        sides,
        jnp.where(chosen, 1.0, 0.0),
        TN,
        precision=lax.Precision.HIGHEST,
        preferred_element_type=jnp.float32,
    )
    for f in (1, 2, 3, 0):
        rate = diffusion_rates[f]
        out = done.at[f]
        out[...] += rate * x_add[:, f * cx : (f + 1) * cx]
        out[pl.ds(0, cy), :] += rate * z_in[0, f]
        out[pl.ds(cells - cy, cy), :] += rate * z_in[1, f]
        out[pl.ds(0, cz, stride=cy), :] += rate * y_in[0, f]
        out[pl.ds(cy - 1, cz, stride=cy), :] += rate * y_in[1, f]
        if f:
            pltpu.make_async_copy(out, outs[f], out_sem.at[f]).start()

    spread_x = jnp.where(same_x, 1.0, 0.0).astype(jnp.bfloat16)
    copies[5].wait()
    settle((n_sec - 1) * n_plane * rows, recv_sem.at[1])

    absorbed = []
    for r in range(rows):
        total = jnp.zeros((1, zone), jnp.float32)
        for k in range(slots):
            tile = jnp.clip(tile_ref[r, k], 0, gathered.shape[0] - 1)
            picked = jnp.where(k < live_ref[r], gathered[tile], 0.0).astype(jnp.bfloat16)
            total += lax.dot_general(picked, matrix[r, k], NT, preferred_element_type=jnp.float32)
        absorbed.append(total)
    absorbed = jnp.concatenate(absorbed, axis=1)
    high = absorbed.astype(jnp.bfloat16).astype(jnp.float32)
    low = absorbed - high
    both = jnp.concatenate(
        [jnp.where(same_r, high, 0.0), jnp.where(same_r, low, 0.0)], axis=0
    ).astype(jnp.bfloat16)
    carried = lax.dot_general(both, spread_x, NT, preferred_element_type=jnp.float32)
    net = carried[: cells // BOX] + carried[cells // BOX :] - box_mean
    source = jnp.broadcast_to(
        net.reshape(cz // BOX, 1, cy, cx), (cz // BOX, BOX, cy, cx)
    ).reshape(cells, cx)
    done[4] = source
    done[0] += heating_rate * source
    for i in (4, 0):
        pltpu.make_async_copy(done.at[i], outs[i], out_sem.at[i]).start()

    settle((n_plane - 1) * rows, send_sem.at[0])
    settle((n_sec - 1) * n_plane * rows, send_sem.at[1])
    for which in (0, 1, 2):
        for side in (0, 1):

            @pl.when(has(which, side))
            def _(which=which, side=side):
                face(which, side).wait_send()

    for i in range(5):
        pltpu.make_async_copy(done.at[i], outs[i], out_sem.at[i]).wait()


def solution(mesh):
    counts = tuple(mesh.shape[a] for a in AXES)

    def local(kelvin, co2, h2o, soot, order, tiles, live, matrix):
        dims = kelvin.shape
        cz, cy, cx = dims
        cells = cz * cy
        rows = matrix.shape[0]
        zone = matrix.shape[2]
        blocks = counts[0] * counts[1] * counts[2] * rows
        flat = [a.reshape(cells, cx) for a in (kelvin, co2, h2o, soot)]
        order = order.reshape(1, -1)
        anywhere = pl.BlockSpec(memory_space=pl.ANY)
        scalars = pl.BlockSpec(memory_space=pltpu.SMEM)
        f32 = jnp.float32
        outs = pl.pallas_call(
            functools.partial(kernel, dims, counts),
            out_shape=[jax.ShapeDtypeStruct((cells, cx), f32)] * 5,
            in_specs=[anywhere] * 5 + [scalars] * 2 + [anywhere],
            out_specs=[anywhere] * 5,
            scratch_shapes=[
                pltpu.VMEM((4, cells, cx), f32),
                pltpu.VMEM(order.shape, jnp.int32),
                pltpu.VMEM(matrix.shape, matrix.dtype),
                pltpu.VMEM((5, cells, cx), f32),
                pltpu.VMEM((blocks, 1, zone), f32),
                pltpu.VMEM((2, 4, cy, cx), f32),
                pltpu.VMEM((2, 4, cz, cx), f32),
                pltpu.VMEM((8, cells), f32),
                pltpu.VMEM((2, 4, cy, cx), f32),
                pltpu.VMEM((2, 4, cz, cx), f32),
                pltpu.VMEM((2, 8, cells), f32),
                pltpu.SemaphoreType.DMA((6,)),
                pltpu.SemaphoreType.DMA((5,)),
                pltpu.SemaphoreType.DMA((3, 2)),
                pltpu.SemaphoreType.DMA((3, 2)),
                pltpu.SemaphoreType.DMA((2,)),
                pltpu.SemaphoreType.DMA((2,)),
            ],
            compiler_params=pltpu.CompilerParams(collective_id=0, has_side_effects=True),
        )(*flat, order, tiles, live, matrix)
        return tuple(o.reshape(dims) for o in outs)

    cell = P("blk", "gy", "sec")
    block = P(AXES)
    return jax.shard_map(
        local,
        mesh=mesh,
        in_specs=(cell,) * 4 + (P("sec", "blk", "gy", None), P(AXES, None), block, P(AXES, None, None, None)),
        out_specs=(cell,) * 5,
        check_vma=False,
    )
```

time: 122 us -> 23.3 us (0.19)
  blocking collectives: 70.7 us -> 0 us
  starting transfers between devices: 15.4 us -> 0 us
  Pallas kernels: 0 us -> 14.6 us
  local copies, waits for them, and re-layouts: 21.2 us -> 7.84 us
  other arithmetic: 11.6 us -> 0 us
  waiting for transfers between devices: 1.45 us -> 0 us
    all_gather x1 -> x0, blocking collectives: 70.7 us -> none  [local(): lax.all_gather(emitted, ('sec', 'blk', 'gy'), axis=0, tiled=True)]
    ppermute x6 -> x0, starting transfers between devices: 15.4 us -> none  [the longest x3 11.5 us: extended(): lax.ppermute(lax.slice_in_dim(block, block.shape[dim] - width, None, axis...]
    pallas_call x0 -> x1, Pallas kernels: none -> 14.6 us  [local(): pl.pallas_call(functools.partial(kernel, dims, counts), out_shape=[jax.Sh...]
    reshape x2 -> x0, local copies, waits for them, and re-layouts: 10.5 us -> none  [the longest x1 5.68 us: local(): radiated_energy_rate.reshape(region_extent_third // BOX, BOX, region_exte...]
    unnamed x23 -> x5, local copies, waits for them, and re-layouts: 0.1 us -> 7.84 us
    add x2 -> x0, other arithmetic: 4.52 us -> none  [the longest x1 3.84 us: diffuse(): return constituent_arrays + rates * (beside - 6.0 * constituent_arrays)]
    another operation x2 -> x0, other arithmetic: 3.6 us -> none  [local(): jnp.stack([normalized_kelvin, co2_molar_part, h2o_molar_part, particulate...]
    gather x1 -> x0, local copies, waits for them, and re-layouts: 3.48 us -> none  [local(): zone_emission = box_emission[box_order]]
  transfers between devices with their start and end apart: 6 -> 0, of which waited for: 1 -> 0; matrix products, arithmetic and copies ran while one was open for 21% -> 0% of each run, Pallas kernels for 0% -> 0%
where the time goes in v1:
time: 23.3 us; the launch traced here: 23.1 us
  Pallas kernels  14.6 us (63%)
  local copies, waits for them, and re-layouts  7.84 us (34%)
  between operations  0.64 us (3%)
    pallas_call x1, Pallas kernels, local(): pl.pallas_call(functools.partial(kernel, dims, counts), out_shape=[jax.Sh...  14.6 us
    unnamed x5, local copies, waits for them, and re-layouts  7.84 us

profile of v1, /device:TPU:0, one launch (start us, length us, event | category | flops | bytes accessed | tf_op | source)
XLA Modules:
  0.0 23.1 jit_solution(2624325121288621483)
XLA Ops:
  0.6 14.6 %shard_map.119 = (f32[256,128]{1,0:T(8,128)}, f32[256,128]{1,0:T(8,128)}, f32[256,128]{1,0:T(8,128)}, f32[256,128]{1,0:T(8,128)}, f32[256,128]{1,0:T(8,128)}) custom-call(f32[256,128]{1,0:T(8,128)} %bitcast.10, f32[256,128]{1,0:T(8,128)} %bitcast.11, f32[256,128]{1,0:T(8,128)} %bitcast.12, f32[256,128]{1,0:T(8,128)} %bitcast.13, s32[1,512]{1,0:T(1,128)} %bitcast.19, ...), custom_call_target="tpu_custom_call" | custom-call | tf_op jit(solution)/shard_map/pallas_call | solution.py:318
  15.2 1.6 %copy.18 = f32[16,16,128]{2,1,0:T(8,128)} copy(f32[16,16,128]{2,1,0:T(8,128)} %bitcast.18) | data formatting | bytes 262144
  16.8 1.6 %copy.19 = f32[16,16,128]{2,1,0:T(8,128)} copy(f32[16,16,128]{2,1,0:T(8,128)} %bitcast.17) | data formatting | bytes 262144
  18.4 1.6 %copy.20 = f32[16,16,128]{2,1,0:T(8,128)} copy(f32[16,16,128]{2,1,0:T(8,128)} %bitcast.16) | data formatting | bytes 262144
  19.9 1.6 %copy.21 = f32[16,16,128]{2,1,0:T(8,128)} copy(f32[16,16,128]{2,1,0:T(8,128)} %bitcast.15) | data formatting | bytes 262144
  21.5 1.6 %copy.22 = f32[16,16,128]{2,1,0:T(8,128)} copy(f32[16,16,128]{2,1,0:T(8,128)} %bitcast.14) | data formatting | bytes 262144

commit v2 on v1

--- a/solution.py
+++ b/solution.py
@@ -55,12 +55,11 @@
     matrix_hbm,
     *rest,
 ):
-    outs = rest[:5]
+    done = rest[0]
     (
         fields,
         order_ref,
         matrix,
-        done,
         gathered,
         z_out,
         y_out,
@@ -69,12 +68,11 @@
         y_in,
         x_in,
         in_sem,
-        out_sem,
         face_send,
         face_recv,
         send_sem,
         recv_sem,
-    ) = rest[5:]
+    ) = rest[1:]
     cz, cy, cx = dims
     n_sec, n_blk, n_gy = counts
     cells = cz * cy
@@ -256,8 +254,6 @@
         out[pl.ds(cells - cy, cy), :] += rate * z_in[1, f]
         out[pl.ds(0, cz, stride=cy), :] += rate * y_in[0, f]
         out[pl.ds(cy - 1, cz, stride=cy), :] += rate * y_in[1, f]
-        if f:
-            pltpu.make_async_copy(out, outs[f], out_sem.at[f]).start()
 
     spread_x = jnp.where(same_x, 1.0, 0.0).astype(jnp.bfloat16)
     copies[5].wait()
@@ -284,8 +280,6 @@
     ).reshape(cells, cx)
     done[4] = source
     done[0] += heating_rate * source
-    for i in (4, 0):
-        pltpu.make_async_copy(done.at[i], outs[i], out_sem.at[i]).start()
 
     settle((n_plane - 1) * rows, send_sem.at[0])
     settle((n_sec - 1) * n_plane * rows, send_sem.at[1])
@@ -296,8 +290,14 @@
             def _(which=which, side=side):
                 face(which, side).wait_send()
 
-    for i in range(5):
-        pltpu.make_async_copy(done.at[i], outs[i], out_sem.at[i]).wait()
+
+def carry(source, *rest):
+    outs, sem = rest[:5], rest[5]
+    copies = [pltpu.make_async_copy(source.at[i], out, sem.at[i]) for i, out in enumerate(outs)]
+    for copy in copies:
+        copy.start()
+    for copy in copies:
+        copy.wait()
 
 
 def solution(mesh):
@@ -315,16 +315,15 @@
         anywhere = pl.BlockSpec(memory_space=pl.ANY)
         scalars = pl.BlockSpec(memory_space=pltpu.SMEM)
         f32 = jnp.float32
-        outs = pl.pallas_call(
+        done = pl.pallas_call(
             functools.partial(kernel, dims, counts),
-            out_shape=[jax.ShapeDtypeStruct((cells, cx), f32)] * 5,
+            out_shape=jax.ShapeDtypeStruct((5, cells, cx), f32),
             in_specs=[anywhere] * 5 + [scalars] * 2 + [anywhere],
-            out_specs=[anywhere] * 5,
+            out_specs=pl.BlockSpec(memory_space=pltpu.VMEM),
             scratch_shapes=[
                 pltpu.VMEM((4, cells, cx), f32),
                 pltpu.VMEM(order.shape, jnp.int32),
                 pltpu.VMEM(matrix.shape, matrix.dtype),
-                pltpu.VMEM((5, cells, cx), f32),
                 pltpu.VMEM((blocks, 1, zone), f32),
                 pltpu.VMEM((2, 4, cy, cx), f32),
                 pltpu.VMEM((2, 4, cz, cx), f32),
@@ -333,7 +332,6 @@
                 pltpu.VMEM((2, 4, cz, cx), f32),
                 pltpu.VMEM((2, 8, cells), f32),
                 pltpu.SemaphoreType.DMA((6,)),
-                pltpu.SemaphoreType.DMA((5,)),
                 pltpu.SemaphoreType.DMA((3, 2)),
                 pltpu.SemaphoreType.DMA((3, 2)),
                 pltpu.SemaphoreType.DMA((2,)),
@@ -341,6 +339,13 @@
             ],
             compiler_params=pltpu.CompilerParams(collective_id=0, has_side_effects=True),
         )(*flat, order, tiles, live, matrix)
+        outs = pl.pallas_call(
+            carry,
+            out_shape=[jax.ShapeDtypeStruct((cells, cx), f32)] * 5,
+            in_specs=[anywhere],
+            out_specs=[anywhere] * 5,
+            scratch_shapes=[pltpu.SemaphoreType.DMA((5,))],
+        )(done)
         return tuple(o.reshape(dims) for o in outs)
 
     cell = P("blk", "gy", "sec")

time: 23.3 us -> 36.5 us (1.57)
  Pallas kernels: 14.6 us -> 35.7 us
  local copies, waits for them, and re-layouts: 7.84 us -> 0 us
    pallas_call x1 -> x2, Pallas kernels: 14.6 us -> 35.7 us  [the longest x1 21 us: local(): pl.pallas_call(carry, out_shape=[jax.ShapeDtypeStruct((cells, cx), f32)]...]
    unnamed x5 -> x0, local copies, waits for them, and re-layouts: 7.84 us -> none
where the time goes in v2:
time: 36.5 us; the launch traced here: 36.3 us
  Pallas kernels  35.7 us (98%)
  between operations  0.64 us (2%)
    pallas_call x1, Pallas kernels, local(): pl.pallas_call(carry, out_shape=[jax.ShapeDtypeStruct((cells, cx), f32)]...  21 us
    pallas_call x1, Pallas kernels, local(): pl.pallas_call(functools.partial(kernel, dims, counts), out_shape=jax.Sha...  14.7 us

profile of v2, /device:TPU:0, one launch (start us, length us, event | category | flops | bytes accessed | tf_op | source)
XLA Modules:
  0.0 36.3 jit_solution(3635528950082875428)
XLA Ops:
  0.6 14.7 %shard_map.119.source = f32[5,256,128]{2,1,0:T(8,128)} custom-call(f32[256,128]{1,0:T(8,128)} %bitcast.10, f32[256,128]{1,0:T(8,128)} %bitcast.11, f32[256,128]{1,0:T(8,128)} %bitcast.12, f32[256,128]{1,0:T(8,128)} %bitcast.13, s32[1,512]{1,0:T(1,128)} %bitcast.14, s32[2,5]{1,0:T(2,128)} %tile_ref.1, s32[2]{0:T(128)} %live_ref.1, ...), custom_call_target="tpu_custom_call" | custom-call | tf_op jit(solution)/shard_map/pallas_call | solution.py:318
  15.3 21.0 %shard_map.120 = (f32[256,128]{1,0:T(8,128)}, f32[256,128]{1,0:T(8,128)}, f32[256,128]{1,0:T(8,128)}, f32[256,128]{1,0:T(8,128)}, f32[256,128]{1,0:T(8,128)}) custom-call(f32[5,256,128]{2,1,0:T(8,128)} %shard_map.119.source), custom_call_target="tpu_custom_call" | custom-call | tf_op jit(solution)/shard_map/pallas_call | solution.py:342

commit v3 on v2

--- a/solution.py
+++ b/solution.py
@@ -84,6 +84,7 @@
     sec, blk, gy = (lax.axis_index(a) for a in AXES)
     plane = blk * n_gy + gy
     me = sec * n_plane + plane
+    n_all = n_sec * n_plane
 
     copies = [
         pltpu.make_async_copy(src, fields.at[i], in_sem.at[i])
@@ -95,11 +96,12 @@
         copy.start()
 
     def plane_peer(i):
-        flat = lax.rem(plane + i, n_plane)
-        return {"blk": lax.div(flat, n_gy), "gy": lax.rem(flat, n_gy)}
-
-    def sec_peer(i):
-        return {"sec": lax.rem(sec + i, n_sec)}
+        flat = lax.rem(me + i, n_all)
+        return {
+            "sec": lax.div(flat, n_plane),
+            "blk": lax.rem(lax.div(flat, n_gy), n_blk),
+            "gy": lax.rem(flat, n_gy),
+        }
 
     def each(count, body):
         if count <= 32:
@@ -109,13 +111,12 @@
             lax.fori_loop(1, count, lambda i, c: (body(i), c)[1], 0)
 
     barrier = pltpu.get_barrier_semaphore()
-    for count, peer in ((n_plane, plane_peer), (n_sec, sec_peer)):
-        each(
-            count,
-            lambda i, peer=peer: pl.semaphore_signal(
-                barrier, inc=1, device_id=peer(i), device_id_type=MESH
-            ),
-        )
+    each(
+        n_all,
+        lambda i: pl.semaphore_signal(
+            barrier, inc=1, device_id=plane_peer(i), device_id_type=MESH
+        ),
+    )
 
     places = (("sec", sec, n_sec), ("blk", blk, n_blk), ("gy", gy, n_gy))
     landing = (x_in, z_in, y_in)
@@ -169,7 +170,7 @@
         packed = jnp.where((lane >> 1) == f, pltpu.roll(field[...], 2 * f + 1, 1), packed)
     x_out[...] = jnp.transpose(packed)[:8]
 
-    pl.semaphore_wait(barrier, n_plane - 1 + n_sec - 1)
+    pl.semaphore_wait(barrier, n_all - 1)
 
     def push(start, length, peer, stage):
         block = gathered.at[pl.ds(start, length)]
@@ -186,7 +187,7 @@
         block = gathered.at[pl.ds(0, length)]
         pltpu.make_async_copy(block, block, sem).wait()
 
-    each(n_plane, lambda i: push(me * rows, rows, plane_peer(i), 0))
+    each(n_all, lambda i: push(me * rows, rows, plane_peer(i), 0))
 
     def face(which, side):
         axis, at, _ = places[which]
@@ -223,9 +224,6 @@
         total += jnp.where(lane < cx - 1, pltpu.roll(value, cx - 1, 1), 0.0)
         done[f] = value + diffusion_rates[f] * (total - 6.0 * value)
 
-    settle((n_plane - 1) * rows, recv_sem.at[0])
-    each(n_sec, lambda i: push(sec * n_plane * rows, n_plane * rows, sec_peer(i), 1))
-
     for which in (0, 1, 2):
         for side in (0, 1):
 
@@ -257,7 +255,7 @@
 
     spread_x = jnp.where(same_x, 1.0, 0.0).astype(jnp.bfloat16)
     copies[5].wait()
-    settle((n_sec - 1) * n_plane * rows, recv_sem.at[1])
+    settle((n_all - 1) * rows, recv_sem.at[0])
 
     absorbed = []
     for r in range(rows):
@@ -281,8 +279,7 @@
     done[4] = source
     done[0] += heating_rate * source
 
-    settle((n_plane - 1) * rows, send_sem.at[0])
-    settle((n_sec - 1) * n_plane * rows, send_sem.at[1])
+    settle((n_all - 1) * rows, send_sem.at[0])
     for which in (0, 1, 2):
         for side in (0, 1):
 
@@ -292,11 +289,19 @@
 
 
 def carry(source, *rest):
-    outs, sem = rest[:5], rest[5]
-    copies = [pltpu.make_async_copy(source.at[i], out, sem.at[i]) for i, out in enumerate(outs)]
-    for copy in copies:
+    outs, held, in_sem, out_sem = rest[:5], *rest[5:]
+    copies_in = [
+        pltpu.make_async_copy(source.at[i], held.at[i], in_sem.at[i]) for i in range(len(outs))
+    ]
+    copies_out = [
+        pltpu.make_async_copy(held.at[i], out, out_sem.at[i]) for i, out in enumerate(outs)
+    ]
+    for copy in copies_in:
         copy.start()
-    for copy in copies:
+    for copy, onward in zip(copies_in, copies_out):
+        copy.wait()
+        onward.start()
+    for copy in copies_out:
         copy.wait()
 
 
@@ -344,7 +349,11 @@
             out_shape=[jax.ShapeDtypeStruct((cells, cx), f32)] * 5,
             in_specs=[anywhere],
             out_specs=[anywhere] * 5,
-            scratch_shapes=[pltpu.SemaphoreType.DMA((5,))],
+            scratch_shapes=[
+                pltpu.VMEM((5, cells, cx), f32),
+                pltpu.SemaphoreType.DMA((5,)),
+                pltpu.SemaphoreType.DMA((5,)),
+            ],
         )(done)
         return tuple(o.reshape(dims) for o in outs)
 

time: 36.5 us -> 16.3 us (0.45)
  Pallas kernels: 35.7 us -> 15.5 us
    pallas_call x1, Pallas kernels: 21 us -> 1.91 us  [local(): pl.pallas_call(carry, out_shape=[jax.ShapeDtypeStruct((cells, cx), f32)]...]
    pallas_call x1, Pallas kernels: 14.7 us -> 13.6 us  [local(): pl.pallas_call(functools.partial(kernel, dims, counts), out_shape=jax.Sha...]
where the time goes in v3:
time: 16.3 us; the launch traced here: 16.2 us
  Pallas kernels  15.5 us (95%)
  between operations  0.64 us (4%)
    pallas_call x1, Pallas kernels, local(): pl.pallas_call(functools.partial(kernel, dims, counts), out_shape=jax.Sha...  13.6 us
    pallas_call x1, Pallas kernels, local(): pl.pallas_call(carry, out_shape=[jax.ShapeDtypeStruct((cells, cx), f32)]...  1.91 us

profile of v3, /device:TPU:0, one launch (start us, length us, event | category | flops | bytes accessed | tf_op | source)
XLA Modules:
  0.0 16.2 jit_solution(2631019005344965158)
XLA Ops:
  0.6 13.6 %shard_map.119.source = f32[5,256,128]{2,1,0:T(8,128)} custom-call(f32[256,128]{1,0:T(8,128)} %bitcast.10, f32[256,128]{1,0:T(8,128)} %bitcast.11, f32[256,128]{1,0:T(8,128)} %bitcast.12, f32[256,128]{1,0:T(8,128)} %bitcast.13, s32[1,512]{1,0:T(1,128)} %bitcast.14, s32[2,5]{1,0:T(2,128)} %tile_ref.1, s32[2]{0:T(128)} %live_ref.1, ...), custom_call_target="tpu_custom_call" | custom-call | tf_op jit(solution)/shard_map/pallas_call | solution.py:323
  14.3 1.9 %shard_map.120 = (f32[256,128]{1,0:T(8,128)}, f32[256,128]{1,0:T(8,128)}, f32[256,128]{1,0:T(8,128)}, f32[256,128]{1,0:T(8,128)}, f32[256,128]{1,0:T(8,128)}) custom-call(f32[5,256,128]{2,1,0:T(8,128)} %shard_map.119.source), custom_call_target="tpu_custom_call" | custom-call | tf_op jit(solution)/shard_map/pallas_call | solution.py:347

commit v4 on v3

--- a/solution.py
+++ b/solution.py
@@ -50,8 +50,8 @@
     h2o_hbm,
     soot_hbm,
     order_hbm,
-    tile_ref,
-    live_ref,
+    tile_hbm,
+    live_hbm,
     matrix_hbm,
     *rest,
 ):
@@ -67,6 +67,8 @@
         z_in,
         y_in,
         x_in,
+        tile_ref,
+        live_ref,
         in_sem,
         face_send,
         face_recv,
@@ -92,6 +94,8 @@
     ]
     copies.append(pltpu.make_async_copy(order_hbm, order_ref, in_sem.at[4]))
     copies.append(pltpu.make_async_copy(matrix_hbm, matrix, in_sem.at[5]))
+    copies.append(pltpu.make_async_copy(tile_hbm, tile_ref, in_sem.at[6]))
+    copies.append(pltpu.make_async_copy(live_hbm, live_ref, in_sem.at[7]))
     for copy in copies:
         copy.start()
 
@@ -254,7 +258,8 @@
         out[pl.ds(cy - 1, cz, stride=cy), :] += rate * y_in[1, f]
 
     spread_x = jnp.where(same_x, 1.0, 0.0).astype(jnp.bfloat16)
-    copies[5].wait()
+    for copy in copies[5:]:
+        copy.wait()
     settle((n_all - 1) * rows, recv_sem.at[0])
 
     absorbed = []
@@ -289,19 +294,11 @@
 
 
 def carry(source, *rest):
-    outs, held, in_sem, out_sem = rest[:5], *rest[5:]
-    copies_in = [
-        pltpu.make_async_copy(source.at[i], held.at[i], in_sem.at[i]) for i in range(len(outs))
-    ]
-    copies_out = [
-        pltpu.make_async_copy(held.at[i], out, out_sem.at[i]) for i, out in enumerate(outs)
-    ]
-    for copy in copies_in:
+    outs, sem = rest[:5], rest[5]
+    copies = [pltpu.make_async_copy(source.at[i], out, sem.at[i]) for i, out in enumerate(outs)]
+    for copy in copies:
         copy.start()
-    for copy, onward in zip(copies_in, copies_out):
-        copy.wait()
-        onward.start()
-    for copy in copies_out:
+    for copy in copies:
         copy.wait()
 
 
@@ -318,12 +315,11 @@
         flat = [a.reshape(cells, cx) for a in (kelvin, co2, h2o, soot)]
         order = order.reshape(1, -1)
         anywhere = pl.BlockSpec(memory_space=pl.ANY)
-        scalars = pl.BlockSpec(memory_space=pltpu.SMEM)
         f32 = jnp.float32
         done = pl.pallas_call(
             functools.partial(kernel, dims, counts),
-            out_shape=jax.ShapeDtypeStruct((5, cells, cx), f32),
-            in_specs=[anywhere] * 5 + [scalars] * 2 + [anywhere],
+            out_shape=pltpu.VMEM((5, cells, cx), f32),
+            in_specs=[anywhere] * 8,
             out_specs=pl.BlockSpec(memory_space=pltpu.VMEM),
             scratch_shapes=[
                 pltpu.VMEM((4, cells, cx), f32),
@@ -336,7 +332,9 @@
                 pltpu.VMEM((2, 4, cy, cx), f32),
                 pltpu.VMEM((2, 4, cz, cx), f32),
                 pltpu.VMEM((2, 8, cells), f32),
-                pltpu.SemaphoreType.DMA((6,)),
+                pltpu.SMEM(tiles.shape, tiles.dtype),
+                pltpu.SMEM(live.shape, live.dtype),
+                pltpu.SemaphoreType.DMA((8,)),
                 pltpu.SemaphoreType.DMA((3, 2)),
                 pltpu.SemaphoreType.DMA((3, 2)),
                 pltpu.SemaphoreType.DMA((2,)),
@@ -350,10 +348,9 @@
             in_specs=[anywhere],
             out_specs=[anywhere] * 5,
             scratch_shapes=[
-                pltpu.VMEM((5, cells, cx), f32),
-                pltpu.SemaphoreType.DMA((5,)),
                 pltpu.SemaphoreType.DMA((5,)),
             ],
+            compiler_params=pltpu.CompilerParams(vmem_limit_bytes=4 << 20),
         )(done)
         return tuple(o.reshape(dims) for o in outs)
 

time: 16.3 us -> 13.8 us (0.85)
  Pallas kernels: 15.5 us -> 13 us
    pallas_call x1, Pallas kernels: 13.6 us -> 12.1 us  [local(): pl.pallas_call(functools.partial(kernel, dims, counts), out_shape=pltpu.V...]
    pallas_call x1, Pallas kernels: 1.91 us -> 0.87 us  [local(): pl.pallas_call(carry, out_shape=[jax.ShapeDtypeStruct((cells, cx), f32)]...]
where the time goes in v4:
time: 13.8 us; the launch traced here: 13.6 us
  Pallas kernels  13 us (94%)
  between operations  0.64 us (5%)
    pallas_call x1, Pallas kernels, local(): pl.pallas_call(functools.partial(kernel, dims, counts), out_shape=pltpu.V...  12.1 us
    pallas_call x1, Pallas kernels, local(): pl.pallas_call(carry, out_shape=[jax.ShapeDtypeStruct((cells, cx), f32)]...  0.87 us

profile of v4, /device:TPU:0, one launch (start us, length us, event | category | flops | bytes accessed | tf_op | source)
XLA Modules:
  0.0 13.6 jit_solution(8969824111169315287)
XLA Ops:
  0.6 12.1 %shard_map.119.source = f32[5,256,128]{2,1,0:T(8,128)S(1)} custom-call(f32[256,128]{1,0:T(8,128)} %bitcast.10, f32[256,128]{1,0:T(8,128)} %bitcast.11, f32[256,128]{1,0:T(8,128)} %bitcast.12, f32[256,128]{1,0:T(8,128)} %bitcast.13, s32[1,512]{1,0:T(1,128)} %bitcast.14, s32[2,5]{1,0:T(2,128)} %tile_hbm.1, s32[2]{0:T(128)} %live_hbm.1, ...), custom_call_target="tpu_custom_call" | custom-call | tf_op jit(solution)/shard_map/pallas_call | solution.py:319
  12.8 0.9 %shard_map.120 = (f32[256,128]{1,0:T(8,128)}, f32[256,128]{1,0:T(8,128)}, f32[256,128]{1,0:T(8,128)}, f32[256,128]{1,0:T(8,128)}, f32[256,128]{1,0:T(8,128)}) custom-call(f32[5,256,128]{2,1,0:T(8,128)S(1)} %shard_map.119.source), custom_call_target="tpu_custom_call" | custom-call | tf_op jit(solution)/shard_map/pallas_call | solution.py:345

commit v5 on v4

--- a/solution.py
+++ b/solution.py
@@ -132,21 +132,7 @@
             def _(land=land, side=side):
                 land[side] = jnp.zeros(land.shape[1:], land.dtype)
 
-    for copy in copies[:5]:
-        copy.wait()
-
-    kelvin = fields[0]
-    vapour = fields[1] + fields[2]
-    soot_kelvin = fields[3] * kelvin
-    share = vapour * (VAPOUR_OFFSET + VAPOUR_SLOPE * kelvin) + (
-        particulate_attenuation_rate * soot_kelvin * (SHARE_OFFSET + SHARE_SLOPE * kelvin)
-    )
-    squared = kelvin * kelvin
-    emission = radiance_multiplier * (squared * squared) * share
-    slabs = emission.reshape(cz // BOX, BOX, cy, cx)
-    slabs = (slabs[:, 0] + slabs[:, 1] + slabs[:, 2] + slabs[:, 3]).reshape(cells // BOX, cx)
-    box_mean = group_sum(group_sum(slabs, 0), 1) * (1.0 / (BOX * BOX * BOX))
-
+    copies[4].wait()
     order = order_ref[...]
     across = cx // BOX
     x_shape = (cx, zones)
@@ -158,6 +144,21 @@
     same_r = lax.div(order, across) == box_row
     pick_x = jnp.where(same_x & (lax.rem(x_at, BOX) == 0), 1.0, 0.0).astype(jnp.bfloat16)
     pick_r = same_r & (lax.rem(r_at, BOX) == 0)
+    for copy in copies[:4]:
+        copy.wait()
+
+    kelvin = fields[0]
+    vapour = fields[1] + fields[2]
+    soot_kelvin = fields[3] * kelvin
+    share = vapour * (VAPOUR_OFFSET + VAPOUR_SLOPE * kelvin) + (
+        particulate_attenuation_rate * soot_kelvin * (SHARE_OFFSET + SHARE_SLOPE * kelvin)
+    )
+    squared = kelvin * kelvin
+    emission = radiance_multiplier * (squared * squared) * share
+    slabs = emission.reshape(cz // BOX, BOX, cy, cx)
+    slabs = (slabs[:, 0] + slabs[:, 1] + slabs[:, 2] + slabs[:, 3]).reshape(cells // BOX, cx)
+    box_mean = group_sum(group_sum(slabs, 0), 1) * (1.0 / (BOX * BOX * BOX))
+
     by_row = jnp.dot(box_mean.astype(jnp.bfloat16), pick_x, preferred_element_type=jnp.float32)
     emitted = jnp.sum(jnp.where(pick_r, by_row, 0.0), axis=0, keepdims=True)
     for r in range(rows):
@@ -235,17 +236,17 @@
             def _(which=which, side=side):
                 face(which, 1 - side).wait_recv()
 
-    shape = (16, 4 * cx)
-    row, column = iota(shape, 0), iota(shape, 1)
+    shape = (32, 4 * cx)
+    row, column = iota(shape, 0) & 15, iota(shape, 1)
     chosen = ((row < 8) & (column == (row >> 1) * cx) & ((row & 1) == 0)) | (
         (row >= 8) & (column == ((row - 8) >> 1) * cx + cx - 1) & ((row & 1) == 1)
     )
     sides = jnp.concatenate([x_in[0], x_in[1]], axis=0)
+    upper = sides.astype(jnp.bfloat16).astype(jnp.float32)
     x_add = lax.dot_general(
-        sides,
+        jnp.concatenate([upper, sides - upper], axis=0),
         jnp.where(chosen, 1.0, 0.0),
         TN,
-        precision=lax.Precision.HIGHEST,
         preferred_element_type=jnp.float32,
     )
     for f in (1, 2, 3, 0):

time: 13.8 us -> 13.4 us (0.971)
  Pallas kernels: 13 us -> 12.6 us
    pallas_call x1, Pallas kernels: 12.1 us -> 11.7 us  [local(): pl.pallas_call(functools.partial(kernel, dims, counts), out_shape=pltpu.V...]
where the time goes in v5:
time: 13.4 us; the launch traced here: 13.2 us
  Pallas kernels  12.6 us (94%)
  between operations  0.64 us (5%)
    pallas_call x1, Pallas kernels, local(): pl.pallas_call(functools.partial(kernel, dims, counts), out_shape=pltpu.V...  11.7 us
    pallas_call x1, Pallas kernels, local(): pl.pallas_call(carry, out_shape=[jax.ShapeDtypeStruct((cells, cx), f32)]...  0.87 us

profile of v5, /device:TPU:0, one launch (start us, length us, event | category | flops | bytes accessed | tf_op | source)
XLA Modules:
  0.0 13.2 jit_solution(8706548653333211912)
XLA Ops:
  0.6 11.7 %shard_map.119.source = f32[5,256,128]{2,1,0:T(8,128)S(1)} custom-call(f32[256,128]{1,0:T(8,128)} %bitcast.10, f32[256,128]{1,0:T(8,128)} %bitcast.11, f32[256,128]{1,0:T(8,128)} %bitcast.12, f32[256,128]{1,0:T(8,128)} %bitcast.13, s32[1,512]{1,0:T(1,128)} %bitcast.14, s32[2,5]{1,0:T(2,128)} %tile_hbm.1, s32[2]{0:T(128)} %live_hbm.1, ...), custom_call_target="tpu_custom_call" | custom-call | tf_op jit(solution)/shard_map/pallas_call | solution.py:320
  12.4 0.9 %shard_map.120 = (f32[256,128]{1,0:T(8,128)}, f32[256,128]{1,0:T(8,128)}, f32[256,128]{1,0:T(8,128)}, f32[256,128]{1,0:T(8,128)}, f32[256,128]{1,0:T(8,128)}) custom-call(f32[5,256,128]{2,1,0:T(8,128)S(1)} %shard_map.119.source), custom_call_target="tpu_custom_call" | custom-call | tf_op jit(solution)/shard_map/pallas_call | solution.py:346
